TPU v7x, 32 devices: a whole 2x2x4 slice. The times are simulated.
32 devices in a mesh: seq: 16 (over z, x, core), exp: 2 (over y).
Axes of the slice: x: 2, y: 2, z: 4, core: 2. Of those that a mesh axis runs over, the one named last changes fastest.
Arguments:
- queries: bfloat16 [1024, 6144], P('seq', 'exp'), may hold values from -6 to 6
- keys: bfloat16 [1024, 6144], P('seq', 'exp'), may hold values from -6 to 6
- values: bfloat16 [1024, 6144], P('seq', 'exp'), may hold values from -6 to 6
- log_decay: float32 [48, 1024], P('exp', 'seq'), may hold values from -1 to 0
- state_in: float32 [48, 128, 128], P('exp'), may hold values from -24 to 24
- norm_gain: float32 [6144], replicated, may hold values from 0.1 to 1.9
- routes: int32 [1024, 2], P('seq'), may hold values from 0 to 7, all different within a row; in each aligned block of 64 rows (0 to 63, 64 to 127, ...) at most 20 rows name the same one
- w_gate: bfloat16 [8, 9216, 6144], P('exp', 'seq'), may hold values from -0.078125 to 0.078125
- w_up: bfloat16 [8, 9216, 6144], P('exp', 'seq'), may hold values from -0.078125 to 0.078125
Outputs:
- expert_hidden: bfloat16 [8, 9216, 320], P('exp', 'seq')
- state_out: float32 [48, 128, 128], P('exp', 'seq')
Inputs may be any that keep to these rules, and one draw needn't show every extreme that they name: `routes`: each token names two different experts; in each aligned block of 64 tokens no expert is named by more than 20 tokens, and some blocks reach exactly 20.
All inputs are finite; a program needn't handle non-finite values.
Results may differ from a plain program's by a relative error of at most 0.0071.
Values may be sent and summed in bfloat16 or wider, within the bound.
No kernel may reach another device: no remote copies, remote signals or barrier semaphores. Data moves between devices by JAX's collectives and lax.ppermute only.
A program may use at most 128 MiB of HBM per device.

v0:
```python
import math

import jax
import jax.numpy as jnp
from jax import lax
from jax.sharding import PartitionSpec as P

CAP = 20


epsilon = 1e-06


def prefix(part, axis, combine, identity):
    place = lax.axis_index(axis)
    gathered = jax.tree.map(lambda a: lax.all_gather(a, axis), part)
    state = jax.tree.map(lambda a, e: jnp.zeros_like(a) + jnp.asarray(e, a.dtype), part, identity)

    def one(hop, state):
        return combine(
            state, jax.tree.map(lambda a: lax.dynamic_index_in_dim(a, hop, 0, False), gathered)
        )

    return lax.fori_loop(0, place, one, state)


def compose(earlier, later_pair):
    return (
        earlier[0] + later_pair[0],
        jnp.exp(later_pair[0])[:, None, None] * earlier[1] + later_pair[1],
    )


def select_rows(routes, expert_ids, capacity, source):
    chosen = jnp.any(routes[None, :, :] == expert_ids[:, None, None], axis=2).astype(jnp.int32)
    position = jnp.cumsum(chosen, axis=1) - 1
    slot_ids = jnp.arange(capacity, dtype=jnp.int32)
    selector = (
        (chosen[:, None, :] == 1) & (position[:, None, :] == slot_ids[None, :, None])
    ).astype(jnp.bfloat16)
    return jnp.einsum("nct,tf->ncf", selector, source, preferred_element_type=jnp.float32).astype(
        jnp.bfloat16
    )


def shards(queries, keys, values, log_decay, state_in, norm_gain, routes, w_gate, w_up):
    length = queries.shape[0]
    features = queries.shape[1]
    local_heads = state_in.shape[0]
    head_dim = state_in.shape[1]
    scaling = 1.0 / math.sqrt(head_dim)
    query_blk = queries.reshape(length, local_heads, head_dim)
    key_blk = keys.reshape(length, local_heads, head_dim)
    value_blk = values.reshape(length, local_heads, head_dim)
    cumlog = jnp.cumsum(log_decay, axis=1)
    block_log = cumlog[:, -1]
    causal = jnp.arange(length)[:, None] >= jnp.arange(length)[None, :]
    scores = (
        jnp.einsum("ihd,jhd->hij", query_blk, key_blk, preferred_element_type=jnp.float32) * scaling
    )
    gap_log = cumlog[:, :, None] - cumlog[:, None, :]
    weights = jnp.where(causal[None], jnp.exp(jnp.where(causal[None], gap_log, 0.0)), 0.0)
    decayed = (scores * weights).astype(jnp.bfloat16)
    inside = jnp.einsum("hij,jhd->ihd", decayed, value_blk, preferred_element_type=jnp.float32)
    key_weighted = key_blk.astype(jnp.float32) * jnp.exp(block_log[:, None] - cumlog).T[:, :, None]
    block_state = jnp.einsum(
        "jhd,jhe->hde", key_weighted, value_blk.astype(jnp.float32), precision=lax.Precision.HIGHEST
    )
    before_log, before_state = prefix(
        (block_log, block_state),
        "seq",
        compose,
        (jnp.zeros_like(block_log), jnp.zeros_like(block_state)),
    )
    entering = jnp.exp(before_log)[:, None, None] * state_in + before_state
    carried_in = jnp.einsum(
        "ihd,hde->ihe",
        query_blk.astype(jnp.float32) * scaling,
        entering,
        precision=lax.Precision.HIGHEST,
    )
    carried_in = carried_in * jnp.exp(cumlog).T[:, :, None]
    attended = (inside + carried_in).astype(jnp.bfloat16).reshape(length, features)
    chain_log = lax.psum(block_log, "seq")
    later_log = chain_log - before_log - block_log
    weighted = jnp.exp(later_log)[:, None, None] * block_state
    reduced = lax.psum_scatter(weighted, "seq", scatter_dimension=1, tiled=True)
    row_count = reduced.shape[1]
    carried_rows = lax.dynamic_slice_in_dim(
        state_in, lax.axis_index("seq") * row_count, row_count, 1
    )
    state_out = reduced + jnp.exp(chain_log)[:, None, None] * carried_rows
    local_experts = w_gate.shape[0]
    gathered = lax.all_gather(attended, "exp", axis=1, tiled=True)
    expert_ids = lax.axis_index("exp") * local_experts + jnp.arange(local_experts, dtype=jnp.int32)
    row_set = select_rows(routes, expert_ids, CAP, gathered)
    row_wide = row_set.astype(jnp.float32)
    normed = (
        row_wide
        * lax.rsqrt(jnp.mean(row_wide * row_wide, axis=2, keepdims=True) + epsilon)
        * norm_gain
    ).astype(jnp.bfloat16)
    block_part = lax.all_gather(normed, "seq", axis=1, tiled=True)
    gate_act = jnp.einsum("efd,end->efn", w_gate, block_part, preferred_element_type=jnp.float32)
    up_act = jnp.einsum("efd,end->efn", w_up, block_part, preferred_element_type=jnp.float32)
    expert_hidden = (jax.nn.silu(gate_act) * up_act).astype(jnp.bfloat16)
    return (expert_hidden, state_out)


def solution(mesh):
    placed = (
        P("seq", "exp"),
        P("seq", "exp"),
        P("seq", "exp"),
        P("exp", "seq"),
        P("exp", None, None),
        P(),
        P("seq", None),
        P("exp", "seq", None),
        P("exp", "seq", None),
    )
    return jax.shard_map(
        shards,
        mesh=mesh,
        in_specs=placed,
        out_specs=(P("exp", "seq", None), P("exp", "seq", None)),
        check_vma=False,
    )
```

profile of v0, /device:TPU:0, one launch (start us, length us, event | category | flops | bytes accessed | tf_op | source)
XLA Modules:
  0.0 444.3 jit_solution(8102716653867087394)
XLA Ops:
  7.2 1.0 reduce_window_sum.23
  8.2 0.2 slice_reduce_fusion
  8.4 0.6 exponential_bitcast_fusion
  9.1 3.8 fusion.29
  12.9 0.0 reduce-scatter.2.cloned.1.call-start
  12.9 0.6 dynamic-slice
  14.2 0.2 dynamic-update-slice
  14.5 36.1 %all-reduce.1 = (f32[384]{0:T(512)S(1)}, f32[24]{0:T(128)}) all-reduce(f32[384]{0:T(512)S(1)} %dynamic-update-slice, f32[24]{0:T(128)S(1)} %slice_reduce_fusion), channel_id=2, replica_groups=mesh['seq'=16,'exp'=2] {'seq'}, use_global_device_ids=true, to_apply=%add | all-reduce | flops 408 | bytes 3264
  50.6 0.7 reshape.72
  51.3 0.1 compare_reduce_fusion
  51.4 0.5 broadcast_compare_fusion
  51.9 0.2 reduce_window_sum.22
  52.1 0.6 iota_compare_fusion.1
  52.7 0.6 broadcast_add_fusion
  53.3 91.2 %all-gather.7.cloned.1.call-done = f32[384,128,128]{2,1,0:T(8,128)} async-done(((f32[24,128,128]{2,1,0:T(8,128)}), f32[384,128,128]{2,1,0:T(8,128)}) %all-gather.7.cloned.1.call-update) | async-done | bytes 25165840 | tf_op jit(solution)/shard_map/all_gather | solution.py:16
  144.5 0.2 broadcast_in_dim.23
  144.8 1.4 fusion.66
  146.1 1.3 broadcast_multiply_fusion
  147.5 0.0 all-gather.5.cloned.1.call-start
  147.5 1.3 copy-done.3
  148.9 3.6 fusion.19
  152.4 1.9 fusion.24
  154.4 0.1 copy.80
  154.5 11.1 %all_gather.18 = bf16[64,6144]{1,0:T(8,128)(2,1)S(1)} all-gather(bf16[64,3072]{1,0:T(8,128)(2,1)S(1)} %bitcast.101), channel_id=1, replica_groups=mesh['seq'=16,'exp'=2] {'exp'}, dimensions={1}, use_global_device_ids=true | all-gather | bytes 1179648 | tf_op jit(solution)/shard_map/all_gather | solution.py:94
  165.5 0.5 multiply_reduce_fusion
  166.1 0.3 multiply_convert_fusion
  166.4 1.7 copy.40
  168.1 75.4 %reduce-scatter.2.cloned.1.call-done = f32[24,8,128]{2,1,0:T(8,128)} async-done(((f32[24,128,128]{2,1,0:T(8,128)}), f32[24,8,128]{2,1,0:T(8,128)}) %reduce-scatter.2.cloned.1.call-update) | async-done | bytes 98320 | tf_op jit(solution)/shard_map/reduce_scatter | solution.py:87
  243.6 1.6 multiply_add_fusion
  245.2 120.3 %all-gather.5.cloned.1.call-done = bf16[4,320,6144]{2,0,1:T(4,128)(2,1)} async-done(((bf16[4,20,6144]{2,0,1:T(4,128)(2,1)}), bf16[4,320,6144]{2,0,1:T(4,128)(2,1)}) %all-gather.5.cloned.1.call-update) | async-done | bytes 15728656 | tf_op jit(solution)/shard_map/all_gather | solution.py:103
  365.5 35.4 %fusion = f32[4,320,576]{2,1,0:T(8,128)} fusion(bf16[4,576,6144]{2,1,0:T(8,128)(2,1)} %param.19, bf16[4,320,6144]{2,0,1:T(4,128)(2,1)} %all-gather.5.cloned.1.call-done), kind=kOutput, calls=%fused_computation.4 | convolution fusion | flops 9059696640 | bytes 46989312 | tf_op jit(solution)/shard_map/efd,end->efn/dot_general | solution.py:105
  400.9 36.8 %fusion.5 = bf16[4,576,320]{1,2,0:T(8,128)(2,1)} fusion(f32[4,320,576]{2,1,0:T(8,128)} %fusion, bf16[4,576,6144]{2,1,0:T(8,128)(2,1)} %param.18, bf16[4,320,6144]{2,0,1:T(4,128)(2,1)} %all-gather.5.cloned.1.call-done), kind=kOutput, calls=%fused_computation.11 | convolution fusion | flops 9064120320 | bytes 48463872 | tf_op jit(solution)/shard_map/efd,end->efn/dot_general | solution.py:104
  (32 shorter events, 0.2 us)
Async XLA Ops:
  7.2 1.9 copy-start
  7.2 5.7 %copy-start.11 = (u32[32]{0:T(128)S(1)}, u32[32]{0:T(128)}, u32[]{:S(2)}) copy-start(u32[32]{0:T(128)} %constant.58) | copy-start | bytes 388
  7.2 44.1 %copy-start.10 = (s32[64,2]{0,1:T(2,128)S(1)}, s32[64,2]{0,1:T(2,128)}, u32[]{:S(2)}) copy-start(s32[64,2]{0,1:T(2,128)} %param.17) | copy-start | bytes 1540
  7.2 137.3 %all-gather.7.cloned.1.call-start = ((), (), s32[]{:S(2)}) async-start(), calls=%async_computation.3 | async-start | bytes 26738688 | tf_op jit(solution)/shard_map/all_gather | solution.py:16
  8.4 136.1 %copy-start.5 = (f32[24]{0:T(128)}, f32[24]{0:T(128)S(1)}, u32[]{:S(2)}) copy-start(f32[24]{0:T(128)S(1)} %slice_reduce_fusion) | copy-start | bytes 292
  12.9 230.7 %reduce-scatter.2.cloned.1.call-start = ((), (), s32[]{:S(2)}) async-start(), calls=%async_computation.2 | async-start | bytes 1671168 | tf_op jit(solution)/shard_map/reduce_scatter | solution.py:87
  144.7 1.4 copy-start.2
  146.1 1.4 copy-start.9
  147.5 1.4 copy-start.3
  147.5 218.0 %all-gather.5.cloned.1.call-start = ((), (), s32[]{:S(2)}) async-start(), calls=%async_computation.1 | async-start | bytes 16711680 | tf_op jit(solution)/shard_map/all_gather | solution.py:103
  152.4 13.1 %copy-start.6 = (s32[4,64]{1,0:T(4,128)S(1)}, s32[4,64]{1,0:T(4,128)}, u32[]{:S(2)}) copy-start(s32[4,64]{1,0:T(4,128)} %broadcast_add_fusion) | copy-start | bytes 3076
  152.4 13.1 %copy-start.8 = (pred[4,64]{1,0:T(4,128)(4,1)S(1)}, pred[4,64]{1,0:T(4,128)(4,1)}, u32[]{:S(2)}) copy-start(pred[4,64]{1,0:T(4,128)(4,1)} %get-tuple-element.59) | copy-start | bytes 772
  154.5 11.6 %copy-start.4 = (f32[6144]{0:T(1024)S(1)}, f32[6144]{0:T(1024)}, u32[]{:S(2)}) copy-start(f32[6144]{0:T(1024)} %param.16) | copy-start | bytes 73732
  166.4 77.2 %copy-start.7 = (f32[24]{0:T(128)S(1)}, f32[24]{0:T(128)}, u32[]{:S(2)}) copy-start(f32[24]{0:T(128)} %get-tuple-element.56) | copy-start | bytes 292
  400.9 36.8 %copy-start.1 = (bf16[64,3072]{1,0:T(8,128)(2,1)S(1)}, bf16[64,3072]{1,0:T(8,128)(2,1)}, u32[]{:S(2)}) copy-start(bf16[64,3072]{1,0:T(8,128)(2,1)} %param.13) | copy-start | bytes 1179652
Sparse Core Ops, SparseCore 0:
  13.0 131.5 all-gather.6
  148.8 94.7 reduce-scatter.1
  246.1 119.3 all-gather.4
where the time goes:
time: 445 us; the launch traced here: 444 us
  waiting for transfers between devices  287 us (64%)
  matrix products  82 us (18%)
  blocking collectives  47.2 us (11%)
  between operations  14.5 us (3%)
  other arithmetic  8.27 us (2%)
  local copies, waits for them, and re-layouts  5.09 us (1%)
    all_gather x1, waiting for transfers between devices, shards(): block_part = lax.all_gather(normed, 'seq', axis=1, tiled=True)  120 us
    all_gather x1, waiting for transfers between devices, prefix(): gathered = jax.tree.map(lambda a: lax.all_gather(a, axis), part)  91.2 us
    reduce_scatter x1, waiting for transfers between devices, shards(): reduced = lax.psum_scatter(weighted, 'seq', scatter_dimension=1, tiled=True)  75.4 us
    dot_general x1, matrix products, shards(): jnp.einsum('efd,end->efn', w_gate, block_part, preferred_element_type=jnp...  36.8 us
    unnamed x1, blocking collectives  36.1 us
    dot_general x1, matrix products, shards(): jnp.einsum('efd,end->efn', w_up, block_part, preferred_element_type=jnp.f...  35.4 us
    all_gather x1, blocking collectives, shards(): gathered = lax.all_gather(attended, 'exp', axis=1, tiled=True)  11.1 us
  transfers between devices with their start and end apart: 3, of which 3 were waited for; matrix products, arithmetic and copies ran while one was open for 3% of the time, Pallas kernels for 0%

commit v1 on v0

v1 whole, which is shorter than its diff:
```python
import functools
import math

import jax
import jax.numpy as jnp
from jax import lax
from jax.experimental import pallas as pl
from jax.experimental.pallas import tpu as pltpu
from jax.sharding import PartitionSpec as P

CAP = 20
EPSILON = 1e-06
COLUMN_PARTS = 3
BLOCKS_A_GROUP = 4
LOG_ROWS = 16
ROUTE_ROW = 6
MIB = 1 << 20


def split_hi_lo(wide):
    hi = wide.astype(jnp.bfloat16)
    return hi, (wide - hi.astype(jnp.float32)).astype(jnp.bfloat16)


def dot_f32(a, b, dims, precision=None):
    return lax.dot_general(
        a, b, (dims, ((), ())), precision=precision, preferred_element_type=jnp.float32
    )


def pack_kernel(place_ref, q_ref, k_ref, v_ref, log_ref, *outs, group, columns):
    block = q_ref.shape[0]
    mine = place_ref[0]
    for hop in range(group):
        message, logs = outs[hop], outs[group + hop]
        dest = jnp.bitwise_xor(mine, hop)
        for part in range(COLUMN_PARTS):
            source = pl.ds(
                pl.multiple_of((part * group + dest) * columns, columns), columns
            )
            target = slice(part * columns, (part + 1) * columns)
            message[0:block, target] = q_ref[:, source]
            message[block : 2 * block, target] = k_ref[:, source]
            message[2 * block : 3 * block, target] = v_ref[:, source]
        logs[...] = log_ref[dest]


def local_kernel(place_ref, *refs, group, heads, head_dim, block):
    messages, logs = refs[:group], refs[group : 2 * group]
    q_out, inside_out, cum_out, state_out, message_out = refs[2 * group : 2 * group + 5]
    k_all, v_all, log_all = refs[2 * group + 5 :]
    mine = place_ref[0]
    length = group * block
    for hop in range(group):
        source = jnp.bitwise_xor(mine, hop)
        rows = pl.ds(pl.multiple_of(source * block, block), block)
        q_out[rows, :] = messages[hop][0:block, :]
        k_all[rows, :] = messages[hop][block : 2 * block, :]
        v_all[rows, :] = messages[hop][2 * block : 3 * block, :]
        log_all[source] = logs[hop][...]
    cumlog = jnp.zeros((log_all.shape[1], length), jnp.float32)
    laid_out = jnp.zeros((log_all.shape[1], length), jnp.float32)
    for at in range(group):
        before = lax.broadcasted_iota(jnp.int32, (block, length), 0) + at * block
        after = lax.broadcasted_iota(jnp.int32, (block, length), 1)
        cumlog = cumlog + dot_f32(
            log_all[at],
            (before <= after).astype(jnp.float32),
            ((1,), (0,)),
            lax.Precision.HIGHEST,
        )
        laid_out = laid_out + dot_f32(
            log_all[at],
            (before == after).astype(jnp.float32),
            ((1,), (0,)),
            lax.Precision.HIGHEST,
        )
    cum_columns = cumlog.T
    cum_out[...] = cum_columns
    scaling = 1.0 / math.sqrt(head_dim)
    causal = lax.broadcasted_iota(jnp.int32, (length, length), 0) >= lax.broadcasted_iota(
        jnp.int32, (length, length), 1
    )
    row_at = lax.broadcasted_iota(jnp.int32, (LOG_ROWS, head_dim), 0)
    for head in range(heads):
        span = slice(head * head_dim, (head + 1) * head_dim)
        query, key, value = q_out[:, span], k_all[:, span], v_all[:, span]
        column = cum_columns[:, head : head + 1]
        row = cumlog[head : head + 1, :]
        total = row[:, length - 1 : length]
        scores = dot_f32(query, key, ((1,), (1,))) * scaling
        weights = jnp.where(causal, jnp.exp(jnp.where(causal, column - row, 0.0)), 0.0)
        decayed = (scores * weights).astype(jnp.bfloat16)
        inside_out[:, span] = dot_f32(decayed, value, ((1,), (0,)))
        weighted = key.astype(jnp.float32) * jnp.exp(total - column)
        hi, lo = split_hi_lo(weighted)
        state = dot_f32(hi, value, ((0,), (0,))) + dot_f32(lo, value, ((0,), (0,)))
        state_out[head] = state
        message_out[head, 0:head_dim, :] = state.astype(jnp.bfloat16)
        wide = jnp.broadcast_to(total, (LOG_ROWS, head_dim))
        first, rest = split_hi_lo(wide)
        left = wide - first.astype(jnp.float32) - rest.astype(jnp.float32)
        pieces = jnp.where(
            row_at == 0,
            first.astype(jnp.float32),
            jnp.where(row_at == 1, rest.astype(jnp.float32), jnp.where(row_at == 2, left, 0.0)),
        )
        if head == 0:
            for choice in range(2):
                for chunk in range(length // head_dim):
                    piece = laid_out[
                        ROUTE_ROW + choice : ROUTE_ROW + choice + 1,
                        chunk * head_dim : (chunk + 1) * head_dim,
                    ]
                    at = 4 + choice * (length // head_dim) + chunk
                    pieces = jnp.where(row_at == at, piece, pieces)
        message_out[head, head_dim : head_dim + LOG_ROWS, :] = pieces.astype(jnp.bfloat16)


def finish_kernel(place_ref, *refs, planes, heads, head_dim):
    arrived = refs[: planes - 1]
    q_ref, inside_ref, cum_ref, own_ref, state_in_ref, gain_ref = refs[planes - 1 : planes + 5]
    outs = refs[planes + 5 :]
    x_outs, final_out = outs[:COLUMN_PARTS], outs[-1]
    plane = place_ref[2]
    a_part = heads // COLUMN_PARTS
    length = q_ref.shape[0]
    scaling = 1.0 / math.sqrt(head_dim)
    squares = jnp.zeros((length, head_dim), jnp.float32)

    def log_of(at, head):
        pieces = arrived[at][head, head_dim : head_dim + LOG_ROWS, :].astype(jnp.float32)
        return pieces[0:1] + pieces[1:2] + pieces[2:3]

    for head in range(heads):
        part, inner = head // a_part, head % a_part
        span = slice(head * head_dim, (head + 1) * head_dim)
        logs = [log_of(at, head) for at in range(planes - 1)]
        states = [arrived[at][head, 0:head_dim, :].astype(jnp.float32) for at in range(planes - 1)]
        passed = jnp.zeros((1, head_dim), jnp.float32)
        entering = jnp.zeros((head_dim, head_dim), jnp.float32)
        for at in range(planes - 1):
            earlier = at + 1 <= plane
            entering = entering + jnp.where(earlier, jnp.exp(passed), 0.0) * states[at]
            passed = passed + jnp.where(earlier, logs[at], 0.0)
        entering = entering + jnp.exp(passed) * state_in_ref[part, 0, inner]
        column = cum_ref[:, head : head + 1]
        own_log = cum_ref[length - 1 : length, head : head + 1]
        running = jnp.exp(own_log) * entering + own_ref[head]
        for at in reversed(range(planes - 1)):
            later = at + 1 > plane
            running = jnp.where(later, jnp.exp(logs[at]), 1.0) * running + jnp.where(
                later, states[at], 0.0
            )
        final_out[head] = running
        hi, lo = split_hi_lo(entering)
        query = q_ref[:, span]
        carried = dot_f32(query, hi, ((1,), (0,))) + dot_f32(query, lo, ((1,), (0,)))
        attended = (inside_ref[:, span] + carried * (jnp.exp(column) * scaling)).astype(
            jnp.bfloat16
        )
        wide = attended.astype(jnp.float32)
        squares = squares + wide * wide
        here = slice(inner * head_dim, (inner + 1) * head_dim)
        x_outs[part][0:length, here] = (wide * gain_ref[0, part, 0, :, here]).astype(jnp.bfloat16)
    sums = jnp.sum(squares, axis=1, keepdims=True)
    row = jnp.broadcast_to(jnp.broadcast_to(sums, (length, head_dim)).T[0:1, :], (LOG_ROWS, length))
    first, rest = split_hi_lo(row)
    first, rest = first.astype(jnp.float32), rest.astype(jnp.float32)
    row_at = lax.broadcasted_iota(jnp.int32, (LOG_ROWS, length), 0)
    left = jnp.where(row_at == 2, row - first - rest, 0.0)
    pieces = jnp.where(row_at == 0, first, jnp.where(row_at == 1, rest, left))
    x_outs[0][length : length + LOG_ROWS, :] = pieces.astype(jnp.bfloat16)


def select_kernel(place_ref, *refs, planes, group, experts, block, length):
    arrived, select_ref, target_ref = refs[:planes], refs[planes], refs[planes + 1]
    exp_at, plane = place_ref[1], place_ref[2]
    chunks = length // arrived[0].shape[2]
    a_select = BLOCKS_A_GROUP // group
    padded = target_ref.shape[1]
    expert_id = lax.broadcasted_iota(jnp.int32, (padded, length), 0) + exp_at * experts
    token = lax.broadcasted_iota(jnp.int32, (padded, length), 1)
    before = lax.broadcasted_iota(jnp.int32, (length, length), 0)
    after = lax.broadcasted_iota(jnp.int32, (length, length), 1)
    counting = ((before <= after) & (before // block == after // block)).astype(jnp.bfloat16)
    for shift in range(planes):
        source = lax.rem(plane - shift + planes, planes)
        pieces = arrived[shift][0].astype(jnp.float32)
        chosen = None
        for choice in range(2):
            named = jnp.concatenate(
                [
                    pieces[4 + choice * chunks + c : 5 + choice * chunks + c]
                    for c in range(chunks)
                ],
                axis=1,
            )
            hit = named.astype(jnp.int32) == expert_id
            chosen = hit if chosen is None else chosen | hit
        count = dot_f32(
            chosen.astype(jnp.float32).astype(jnp.bfloat16), counting, ((1,), (0,))
        ).astype(jnp.int32)
        in_select = lax.rem(source, a_select) * group + token // block
        target_ref[source] = jnp.where(chosen, in_select * CAP + count - 1, -1)
    slots = BLOCKS_A_GROUP * CAP
    slot = lax.broadcasted_iota(jnp.int32, (slots, a_select * length), 0)
    for at in range(planes // a_select):
        target = jnp.concatenate(
            [target_ref[at * a_select + i] for i in range(a_select)], axis=1
        )
        for expert in range(experts):
            select_ref[at, expert * slots : (expert + 1) * slots, :] = (
                (target[expert : expert + 1] == slot).astype(jnp.float32).astype(jnp.bfloat16)
            )


def expert_kernel(place_ref, x_ref, select_ref, gate_ref, up_ref, *refs, part, first, last):
    refs = list(refs)
    acc_in = None if first else refs.pop(0)
    scale_ref = refs.pop(0) if last else None
    out, rows_scratch, weights, acc, sems = refs
    expert, half = pl.program_id(0), pl.program_id(1)
    experts, halves = pl.num_programs(0), pl.num_programs(1)
    n_experts = rows_scratch.shape[0]
    group = x_ref.shape[1]
    length, columns = x_ref.shape[3], x_ref.shape[4]
    n_select, select_rows, select_tokens = select_ref.shape
    a_select = select_tokens // length
    slots = select_rows // n_experts
    hidden = gate_ref.shape[1]
    padded, depth = weights.shape[1] // 2, weights.shape[2]
    step = expert * halves + half
    slot = lax.rem(step, 2)

    def copies(step, slot):
        of_expert, of_half = step // halves, lax.rem(step, halves)
        block = jnp.bitwise_xor(of_half, place_ref[1]) * COLUMN_PARTS + part
        span = pl.ds(pl.multiple_of(block * depth, depth), depth)
        return [
            pltpu.make_async_copy(
                ref.at[of_expert, :, span],
                weights.at[slot, at * padded : at * padded + hidden],
                sems.at[slot, at],
            )
            for at, ref in enumerate((gate_ref, up_ref))
        ]

    @pl.when(step == 0)
    def _():
        for copy in copies(step, slot):
            copy.start()
        if padded > hidden:
            empty = jnp.zeros((2, padded - hidden, depth), jnp.bfloat16)
            weights[:, hidden:padded] = empty
            weights[:, padded + hidden : 2 * padded] = empty

    @pl.when(step + 1 < experts * halves)
    def _():
        for copy in copies(step + 1, 1 - slot):
            copy.start()

    @pl.when(expert == 0)
    def _():
        for at in range(n_select):
            for member in range(group):
                tokens = x_ref[at * a_select : (at + 1) * a_select, member, 0].reshape(
                    select_tokens, columns
                )
                picked = dot_f32(select_ref[at], tokens, ((1,), (0,))).astype(jnp.bfloat16)
                for e in range(n_experts):
                    rows_scratch[
                        e,
                        half,
                        at * slots : (at + 1) * slots,
                        member * columns : (member + 1) * columns,
                    ] = picked[e * slots : (e + 1) * slots]

    for copy in copies(step, slot):
        copy.wait()
    sums = dot_f32(rows_scratch[expert, half], weights[slot], ((1,), (1,)))

    @pl.when(half == 0)
    def _():
        acc[...] = sums if first else acc_in[0] + sums

    @pl.when(half > 0)
    def _():
        acc[...] += sums

    @pl.when(half == halves - 1)
    def _():
        if last:
            scale = scale_ref[0]
            gate = acc[:, 0:hidden] * scale
            up = acc[:, padded : padded + hidden] * scale
            out[0] = (gate / (1.0 + jnp.exp(-gate)) * up).astype(jnp.bfloat16)
        else:
            out[0] = acc[...]


def vmem_spec():
    return pl.BlockSpec(memory_space=pltpu.VMEM)


def smem_spec():
    return pl.BlockSpec(memory_space=pltpu.SMEM)


def expert_part(part, place, x, select, w_gate, w_up, acc, scale):
    first, last = acc is None, scale is not None
    experts, hidden, width = w_gate.shape
    planes, group, halves, _, columns = x.shape
    length = select.shape[2] * select.shape[0] // planes
    depth = group * columns
    n_rows = select.shape[0] * select.shape[1] // experts
    padded = -(-hidden // 128) * 128
    acc_spec = pl.BlockSpec((1, n_rows, 2 * padded), lambda e, half: (e, 0, 0))
    anywhere = pl.BlockSpec(memory_space=pl.ANY)
    in_specs = [
        smem_spec(),
        pl.BlockSpec(
            (planes, group, 1, length, columns),
            lambda e, half: (0, 0, jnp.where(e == 0, half, halves - 1), 0, 0),
        ),
        pl.BlockSpec(select.shape, lambda e, half: (0, 0, 0)),
        anywhere,
        anywhere,
    ]
    operands = [place, x, select, w_gate, w_up]
    aliases = {}
    if not first:
        in_specs.append(acc_spec)
        operands.append(acc)
    if last:
        in_specs.append(pl.BlockSpec((1, n_rows, 1), lambda e, half: (e, 0, 0)))
        operands.append(scale)
        out_shape = jax.ShapeDtypeStruct((experts, n_rows, hidden), jnp.bfloat16)
        out_spec = pl.BlockSpec((1, n_rows, hidden), lambda e, half: (e, 0, 0))
    else:
        out_shape = jax.ShapeDtypeStruct((experts, n_rows, 2 * padded), jnp.float32)
        out_spec = acc_spec
        if not first:
            aliases = {5: 0}
    return pl.pallas_call(
        functools.partial(expert_kernel, part=part, first=first, last=last),
        grid=(experts, halves),
        in_specs=in_specs,
        out_specs=out_spec,
        out_shape=out_shape,
        input_output_aliases=aliases,
        scratch_shapes=[
            pltpu.VMEM((experts, halves, n_rows, depth), jnp.bfloat16),
            pltpu.VMEM((2, 2 * padded, depth), jnp.bfloat16),
            pltpu.VMEM((n_rows, 2 * padded), jnp.float32),
            pltpu.SemaphoreType.DMA((2, 2)),
        ],
        compiler_params=pltpu.CompilerParams(vmem_limit_bytes=56 * MIB),
        cost_estimate=pl.CostEstimate(
            flops=4 * experts * hidden * n_rows * depth * halves,
            bytes_accessed=4 * experts * hidden * depth * halves,
            transcendentals=0,
        ),
        name="expert_part",
    )(*operands)


def shards(queries, keys, values, log_decay, state_in, norm_gain, routes, w_gate, w_up, *, shape):
    n_seq, n_exp = shape["seq"], shape["exp"]
    block, features = queries.shape
    local_heads, head_dim = state_in.shape[0], state_in.shape[1]
    group = next(
        g for g in (4, 2, 1) if local_heads % (g * COLUMN_PARTS) == 0 and n_seq % g == 0
    )
    planes = n_seq // group
    heads = local_heads // group
    a_part = heads // COLUMN_PARTS
    columns = a_part * head_dim
    length = group * block
    width = heads * head_dim
    seq_at = lax.axis_index("seq")
    exp_at = lax.axis_index("exp")
    member_at = seq_at % group
    plane_at = seq_at // group
    place = jnp.stack([member_at, exp_at, plane_at]).astype(jnp.int32)

    def to_member(a, hop):
        if hop == 0:
            return a
        pairs = [(s, s // group * group + ((s % group) ^ hop)) for s in range(n_seq)]
        return lax.ppermute(a, "seq", pairs)

    def to_plane(a, shift):
        pairs = [((s), (s // group + shift) % planes * group + s % group) for s in range(n_seq)]
        return lax.ppermute(a, "seq", pairs)

    by_member = log_decay.reshape(COLUMN_PARTS, group, a_part, block).transpose(1, 0, 2, 3)
    by_member = by_member.reshape(group, heads, block)
    by_member = jnp.pad(by_member, ((0, 0), (0, ROUTE_ROW - heads), (0, 0)))
    named = jnp.broadcast_to(routes.T.astype(jnp.float32)[None], (group, 2, block))
    by_member = jnp.concatenate([by_member, named], axis=1)
    smem = smem_spec()
    packed = pl.pallas_call(
        functools.partial(pack_kernel, group=group, columns=columns),
        in_specs=[smem] + [vmem_spec()] * 4,
        out_specs=[vmem_spec()] * (2 * group),
        out_shape=[jax.ShapeDtypeStruct((3 * block, width), jnp.bfloat16)] * group
        + [jax.ShapeDtypeStruct((8, block), jnp.float32)] * group,
        compiler_params=pltpu.CompilerParams(vmem_limit_bytes=16 * MIB),
        name="pack",
    )(place, queries, keys, values, by_member)
    messages = [to_member(packed[hop], hop) for hop in range(group)]
    logs = [to_member(packed[group + hop], hop) for hop in range(group)]

    query, inside, cumlog, own_state, message = pl.pallas_call(
        functools.partial(
            local_kernel, group=group, heads=heads, head_dim=head_dim, block=block
        ),
        in_specs=[smem] + [vmem_spec()] * (2 * group),
        out_specs=[vmem_spec()] * 5,
        out_shape=[
            jax.ShapeDtypeStruct((length, width), jnp.bfloat16),
            jax.ShapeDtypeStruct((length, width), jnp.float32),
            jax.ShapeDtypeStruct((length, 8), jnp.float32),
            jax.ShapeDtypeStruct((heads, head_dim, head_dim), jnp.float32),
            jax.ShapeDtypeStruct((heads, head_dim + LOG_ROWS, head_dim), jnp.bfloat16),
        ],
        scratch_shapes=[
            pltpu.VMEM((length, width), jnp.bfloat16),
            pltpu.VMEM((length, width), jnp.bfloat16),
            pltpu.VMEM((group, 8, block), jnp.float32),
        ],
        compiler_params=pltpu.CompilerParams(vmem_limit_bytes=24 * MIB),
        name="local_attention",
    )(place, *messages, *logs)
    arrived = [to_plane(message, shift) for shift in range(1, planes)]

    experts = w_gate.shape[0]
    slots = BLOCKS_A_GROUP * CAP
    n_select = n_seq // BLOCKS_A_GROUP
    routes_spec = pl.BlockSpec(
        (1, LOG_ROWS, head_dim), lambda i, place: (0, head_dim // LOG_ROWS, 0)
    )
    select = pl.pallas_call(
        functools.partial(
            select_kernel,
            planes=planes,
            group=group,
            experts=experts,
            block=block,
            length=length,
        ),
        grid_spec=pltpu.PrefetchScalarGridSpec(
            num_scalar_prefetch=1,
            grid=(1,),
            in_specs=[routes_spec] * planes,
            out_specs=pl.BlockSpec(
                (n_select, experts * slots, BLOCKS_A_GROUP * block), lambda i, place: (0, 0, 0)
            ),
            scratch_shapes=[pltpu.VMEM((planes, 8, length), jnp.int32)],
        ),
        out_shape=jax.ShapeDtypeStruct(
            (n_select, experts * slots, BLOCKS_A_GROUP * block), jnp.bfloat16
        ),
        compiler_params=pltpu.CompilerParams(vmem_limit_bytes=16 * MIB),
        name="select_rows",
    )(place, message, *arrived)

    part_rows = [length + LOG_ROWS] + [length] * (COLUMN_PARTS - 1)
    whole = lambda *dims: pl.BlockSpec(dims, lambda i, place: (0,) * len(dims))
    state_blocks = state_in.reshape(COLUMN_PARTS, group, a_part, head_dim, head_dim)
    gain_blocks = norm_gain.reshape(n_exp, COLUMN_PARTS, group, 1, columns)
    finished = pl.pallas_call(
        functools.partial(finish_kernel, planes=planes, heads=heads, head_dim=head_dim),
        grid_spec=pltpu.PrefetchScalarGridSpec(
            num_scalar_prefetch=1,
            grid=(1,),
            in_specs=[whole(heads, head_dim + LOG_ROWS, head_dim)] * (planes - 1)
            + [
                whole(length, width),
                whole(length, width),
                whole(length, 8),
                whole(heads, head_dim, head_dim),
                pl.BlockSpec(
                    (COLUMN_PARTS, 1, a_part, head_dim, head_dim),
                    lambda i, place: (0, place[0], 0, 0, 0),
                ),
                pl.BlockSpec(
                    (1, COLUMN_PARTS, 1, 1, columns),
                    lambda i, place: (place[1], 0, place[0], 0, 0),
                ),
            ],
            out_specs=[whole(n_tokens, columns) for n_tokens in part_rows]
            + [whole(heads, head_dim, head_dim)],
        ),
        out_shape=[
            jax.ShapeDtypeStruct((n_tokens, columns), jnp.bfloat16) for n_tokens in part_rows
        ]
        + [jax.ShapeDtypeStruct((heads, head_dim, head_dim), jnp.float32)],
        compiler_params=pltpu.CompilerParams(vmem_limit_bytes=32 * MIB),
        name="finish_attention",
    )(place, *arrived, query, inside, cumlog, own_state, state_blocks, gain_blocks)
    x_parts, final = finished[:COLUMN_PARTS], finished[-1]

    def to_half(a, hop):
        if hop == 0:
            return a
        return lax.ppermute(a, "exp", [(e, e ^ hop) for e in range(n_exp)])

    gathered = []
    for x in x_parts:
        halves = jnp.stack([to_half(x, hop) for hop in range(n_exp)])
        gathered.append(
            lax.all_gather(halves, "seq").reshape(planes, group, n_exp, x.shape[0], columns)
        )
    pieces = gathered[0][:, :, :, length : length + 3, :].astype(jnp.float32)
    mean = jnp.sum(pieces, axis=(1, 2, 3)) / (n_exp * features)
    token_scale = lax.rsqrt(mean + EPSILON).reshape(n_select, 1, BLOCKS_A_GROUP * block)
    slot_scale = jnp.sum(select.astype(jnp.float32) * token_scale, axis=2)
    slot_scale = slot_scale.reshape(n_select, experts, slots).transpose(1, 0, 2)
    slot_scale = slot_scale.reshape(experts, n_select * slots, 1)

    acc = None
    for part in range(COLUMN_PARTS):
        scale = slot_scale if part == COLUMN_PARTS - 1 else None
        acc = expert_part(part, place, gathered[part], select, w_gate, w_up, acc, scale)
    hidden = acc.swapaxes(1, 2)

    out_rows = head_dim // n_seq
    pieces = []
    for hop in range(group):
        dest = plane_at * group + jnp.bitwise_xor(member_at, hop)
        piece = lax.dynamic_slice_in_dim(final, dest * out_rows, out_rows, 1)
        pieces.append(to_member(piece, hop))
    stacked = jnp.stack(pieces)
    ordered = [
        lax.dynamic_index_in_dim(stacked, jnp.bitwise_xor(member_at, m), 0, False)
        for m in range(group)
    ]
    ordered = [a.reshape(COLUMN_PARTS, a_part, out_rows, head_dim) for a in ordered]
    state_out = jnp.stack(ordered, axis=1).reshape(local_heads, out_rows, head_dim)
    return (hidden, state_out)


def solution(mesh):
    placed = (
        P("seq", "exp"),
        P("seq", "exp"),
        P("seq", "exp"),
        P("exp", "seq"),
        P("exp", None, None),
        P(),
        P("seq", None),
        P("exp", "seq", None),
        P("exp", "seq", None),
    )
    return jax.shard_map(
        functools.partial(shards, shape=dict(mesh.shape)),
        mesh=mesh,
        in_specs=placed,
        out_specs=(P("exp", "seq", None), P("exp", "seq", None)),
        check_vma=False,
    )
```

time: 445 us -> 246 us (0.55)
  waiting for transfers between devices: 287 us -> 138 us
  matrix products: 82 us -> 0 us
  Pallas kernels: 0 us -> 62.8 us
  blocking collectives: 47.2 us -> 0 us
  starting transfers between devices: 0.12 us -> 18.8 us
    all_gather x2 -> x3, waiting for transfers between devices: 212 us -> 99.4 us  [shards(): lax.all_gather(halves, 'seq')]
    dot_general x6 -> x0, matrix products: 82 us -> none  [the longest x1 36.8 us: shards(): jnp.einsum('efd,end->efn', w_gate, block_part, preferred_element_type=jnp...]
    reduce_scatter x1 -> x0, waiting for transfers between devices: 75.4 us -> none  [shards(): reduced = lax.psum_scatter(weighted, 'seq', scatter_dimension=1, tiled=True)]
    pallas_call x0 -> x7, Pallas kernels: none -> 62.8 us  [the longest x3 57 us: expert_part(): pl.pallas_call(functools.partial(expert_kernel, part=part, first=first, l...]
    ppermute x0 -> x15, waiting for transfers between devices: none -> 38.1 us  [the longest x9 13.8 us: to_member(): return lax.ppermute(a, 'seq', pairs)]
    unnamed x1 -> x0, blocking collectives: 36.1 us -> none
    ppermute x0 -> x15, starting transfers between devices: none -> 18.5 us  [the longest x9 7.92 us: to_member(): return lax.ppermute(a, 'seq', pairs)]
    all_gather x1 -> x0, blocking collectives: 11.1 us -> none  [shards(): gathered = lax.all_gather(attended, 'exp', axis=1, tiled=True)]
  transfers between devices with their start and end apart: 3 -> 18, of which waited for: 3 -> 11; matrix products, arithmetic and copies ran while one was open for 3% -> 2% of each run, Pallas kernels for 0% -> 16%
where the time goes in v1:
time: 246 us; the launch traced here: 245 us
  waiting for transfers between devices  138 us (56%)
  Pallas kernels  62.8 us (26%)
  starting transfers between devices  18.8 us (8%)
  between operations  13.9 us (6%)
  local copies, waits for them, and re-layouts  7.11 us (3%)
  other arithmetic  4.87 us (2%)
    all_gather x3, waiting for transfers between devices, shards(): lax.all_gather(halves, 'seq')  99.4 us
    pallas_call x3, Pallas kernels, expert_part(): pl.pallas_call(functools.partial(expert_kernel, part=part, first=first, l...  57 us
    ppermute x9, waiting for transfers between devices, to_member(): return lax.ppermute(a, 'seq', pairs)  13.8 us
    ppermute x3, waiting for transfers between devices, to_plane(): return lax.ppermute(a, 'seq', pairs)  13.4 us
    ppermute x3, waiting for transfers between devices, to_half(): return lax.ppermute(a, 'exp', [(e, e ^ hop) for e in range(n_exp)])  10.9 us
    ppermute x9, starting transfers between devices, to_member(): return lax.ppermute(a, 'seq', pairs)  7.92 us
    ppermute x3, starting transfers between devices, to_plane(): return lax.ppermute(a, 'seq', pairs)  5.83 us
    unnamed x14, local copies, waits for them, and re-layouts  5.14 us
  transfers between devices with their start and end apart: 18, of which 11 were waited for; matrix products, arithmetic and copies ran while one was open for 2% of the time, Pallas kernels for 16%

profile of v1, /device:TPU:0, one launch (start us, length us, event | category | flops | bytes accessed | tf_op | source)
XLA Modules:
  0.0 245.1 jit_solution(6587487942995441322)
XLA Ops:
  8.7 1.0 copy-done.2
  9.7 1.0 copy-done.3
  10.7 1.0 copy-done.4
  12.9 2.6 %collective-permute-start.1 = (bf16[192,768]{1,0:T(8,128)(2,1)S(1)}, bf16[192,768]{1,0:T(8,128)(2,1)S(1)}, u32[]{:S(2)}, u32[]{:S(2)}) collective-permute-start(bf16[192,768]{1,0:T(8,128)(2,1)S(1)} %get-tuple-element.21), channel_id=1, source_target_pairs={{0,4},{2,6},{4,0},{6,2},{8,12},{10,14},{12,8},{14,10},{16,20},{18,... | collective-permute-start | bytes 884744 | tf_op jit(solution)/shard_map/ppermute | solution.py:391
  15.7 1.9 collective-permute-start.4
  18.4 11.1 %collective-permute-done.4.refs_6_ = f32[8,64]{1,0:T(8,128)S(1)} collective-permute-done((f32[8,64]{1,0:T(8,128)S(1)}, f32[8,64]{1,0:T(8,128)S(1)}, u32[]{:S(2)}, u32[]{:S(2)}) %collective-permute-start.4) | collective-permute-done | bytes 2080 | tf_op jit(solution)/shard_map/ppermute | solution.py:391
  29.6 2.7 %local_attention.1 = (bf16[256,768]{1,0:T(8,128)(2,1)S(1)}, f32[256,768]{1,0:T(8,128)S(1)}, f32[256,8]{1,0:T(8,128)S(1)}, f32[6,128,128]{2,1,0:T(8,128)S(1)}, bf16[6,144,128]{2,1,0:T(8,128)(2,1)S(1)}) custom-call(s32[3]{0:T(128)S(1)} %pad_add_fusion.place_ref, bf16[192,768]{1,0:T(8,128)(2,1)S(1)} %get-tuple-element.19.refs_0_, ...), custom_call_target="tpu_custom_call" | custom-call | tf_op jit(solution)/shard_map/local_attention/pallas_call | solution.py:415
  32.3 1.9 collective-permute-start.6
  34.2 2.6 %collective-permute-start.7 = (bf16[6,144,128]{2,1,0:T(8,128)(2,1)S(1)}, bf16[6,144,128]{2,1,0:T(8,128)(2,1)S(1)}, u32[]{:S(2)}, u32[]{:S(2)}) collective-permute-start(bf16[6,144,128]{2,1,0:T(8,128)(2,1)S(1)} %get-tuple-element.27.refs_0_), channel_id=1, source_target_pairs={{0,16},{2,18},{4,20},{6,22},{8,24},{10,26},{12,28},{14,30},{16,0},... | collective-permute-start | bytes 663560 | tf_op jit(solution)/shard_map/ppermute | solution.py:395
  36.8 1.4 collective-permute-start.8
  38.2 4.4 %collective-permute-done.6.refs_0_.refs_1_ = bf16[6,144,128]{2,1,0:T(8,128)(2,1)S(1)} collective-permute-done((bf16[6,144,128]{2,1,0:T(8,128)(2,1)S(1)}, bf16[6,144,128]{2,1,0:T(8,128)(2,1)S(1)}, u32[]{:S(2)}, u32[]{:S(2)}) %collective-permute-start.6) | collective-permute-done | bytes 221216 | tf_op jit(solution)/shard_map/ppermute | solution.py:395
  42.6 9.0 %collective-permute-done.7.refs_1_.refs_2_ = bf16[6,144,128]{2,1,0:T(8,128)(2,1)S(1)} collective-permute-done((bf16[6,144,128]{2,1,0:T(8,128)(2,1)S(1)}, bf16[6,144,128]{2,1,0:T(8,128)(2,1)S(1)}, u32[]{:S(2)}, u32[]{:S(2)}) %collective-permute-start.7) | collective-permute-done | bytes 221216 | tf_op jit(solution)/shard_map/ppermute | solution.py:395
  51.6 1.4 copy-done.1
  53.7 1.5 finish_attention.1
  55.2 1.6 collective-permute-start.11
  56.8 4.0 %collective-permute-done.11 = bf16[272,256]{1,0:T(8,128)(2,1)S(1)} collective-permute-done((bf16[272,256]{1,0:T(8,128)(2,1)S(1)}, bf16[272,256]{1,0:T(8,128)(2,1)S(1)}, u32[]{:S(2)}, u32[]{:S(2)}) %collective-permute-start.11) | collective-permute-done | bytes 139296 | tf_op jit(solution)/shard_map/ppermute | solution.py:508
  61.5 1.6 collective-permute-start.10
  63.1 3.4 %collective-permute-done.10 = bf16[256,256]{1,0:T(8,128)(2,1)S(1)} collective-permute-done((bf16[256,256]{1,0:T(8,128)(2,1)S(1)}, bf16[256,256]{1,0:T(8,128)(2,1)S(1)}, u32[]{:S(2)}, u32[]{:S(2)}) %collective-permute-start.10) | collective-permute-done | bytes 131104 | tf_op jit(solution)/shard_map/ppermute | solution.py:508
  67.6 1.6 collective-permute-start.9
  69.2 3.4 %collective-permute-done.9 = bf16[256,256]{1,0:T(8,128)(2,1)S(1)} collective-permute-done((bf16[256,256]{1,0:T(8,128)(2,1)S(1)}, bf16[256,256]{1,0:T(8,128)(2,1)S(1)}, u32[]{:S(2)}, u32[]{:S(2)}) %collective-permute-start.9) | collective-permute-done | bytes 131104 | tf_op jit(solution)/shard_map/ppermute | solution.py:508
  73.5 1.6 collective-permute-start.13
  75.4 0.9 select_rows.1.select_ref
  76.3 1.4 collective-permute-done.13
  77.7 1.3 collective-permute-done.14
  79.6 37.4 %all-gather.11.cloned.1.call-done = bf16[32,272,256]{2,1,0:T(8,128)(2,1)} async-done(((bf16[2,272,256]{2,1,0:T(8,128)(2,1)}), bf16[32,272,256]{2,1,0:T(8,128)(2,1)}) %all-gather.11.cloned.1.call-update) | async-done | bytes 4456464 | tf_op jit(solution)/shard_map/all_gather | solution.py:514
  117.0 0.9 convert_reduce_fusion
  118.4 1.1 reshape.61.refs_1_
  119.5 18.8 %expert_part.3.refs_0_ = f32[4,320,1280]{2,1,0:T(8,128)} custom-call(s32[3]{0:T(128)} %copy-done.5, bf16[4,4,2,272,256]{4,3,2,1,0:T(8,128)(2,1)} %bitcast.38, bf16[4,320,256]{2,1,0:T(8,128)(2,1)} %copy-done, bf16[4,576,6144]{2,1,0:T(8,128)(2,1)} %gate_ref.5, bf16[4,576,6144]{2,1,0:T(8,128)(2,1)} %up_ref.5), custom_call_target="tpu_custom_call" | custom-call | flops 6039797760 | bytes 18874368 | tf_op jit(solution)/shard_map/expert_part/pallas_call | solution.py:345
  138.4 30.1 %all-gather.9.cloned.1.call-done = bf16[32,256,256]{2,1,0:T(8,128)(2,1)} async-done(((bf16[2,256,256]{2,1,0:T(8,128)(2,1)}), bf16[32,256,256]{2,1,0:T(8,128)(2,1)}) %all-gather.9.cloned.1.call-update) | async-done | bytes 4194320 | tf_op jit(solution)/shard_map/all_gather | solution.py:514
  168.4 19.5 %expert_part.4.refs_0_ = f32[4,320,1280]{2,1,0:T(8,128)} custom-call(s32[3]{0:T(128)} %copy-done.5, bf16[4,4,2,256,256]{4,3,2,1,0:T(8,128)(2,1)} %bitcast.39, bf16[4,320,256]{2,1,0:T(8,128)(2,1)} %copy-done, bf16[4,576,6144]{2,1,0:T(8,128)(2,1)} %gate_ref.5, bf16[4,576,6144]{2,1,0:T(8,128)(2,1)} %up_ref.5, ...), custom_call_target="tpu_custom_call", output_to_operand_aliasing={{}: (5, {})} | custom-call | flops 6039797760 | bytes 18874368 | tf_op jit(solution)/shard_map/expert_part/pallas_call | solution.py:345
  187.9 31.9 %all-gather.7.cloned.1.call-done = bf16[32,256,256]{2,1,0:T(8,128)(2,1)} async-done(((bf16[2,256,256]{2,1,0:T(8,128)(2,1)}), bf16[32,256,256]{2,1,0:T(8,128)(2,1)}) %all-gather.7.cloned.1.call-update) | async-done | bytes 4194320 | tf_op jit(solution)/shard_map/all_gather | solution.py:514
  219.8 18.7 %expert_part.5 = bf16[4,320,576]{2,1,0:T(8,128)(2,1)} custom-call(s32[3]{0:T(128)} %copy-done.5, bf16[4,4,2,256,256]{4,3,2,1,0:T(8,128)(2,1)} %bitcast.40, bf16[4,320,256]{2,1,0:T(8,128)(2,1)} %copy-done, bf16[4,576,6144]{2,1,0:T(8,128)(2,1)} %gate_ref.5, bf16[4,576,6144]{2,1,0:T(8,128)(2,1)} %up_ref.5, f32[4,320,1280]{2,1,0:T(8,128)} %expert_part.4.refs_0_, ...), custom_call_target="tpu_custom_call" | custom-call | flops 6039797760 | bytes 18874368 | tf_op jit(solution)/shard_map/expert_part/pallas_call | solution.py:345
  (47 shorter events, 8.5 us)
Async XLA Ops:
  7.2 109.9 %all-gather.11.cloned.1.call-start = ((), (), s32[]{:S(2)}) async-start(), calls=%async_computation.2 | async-start | bytes 4734976 | tf_op jit(solution)/shard_map/all_gather | solution.py:514
  8.7 1.0 copy-start.2
  9.7 1.0 copy-start.3
  10.7 1.0 copy-start.4
  11.7 63.6 %copy-start.5 = (s32[3]{0:T(128)}, s32[3]{0:T(128)S(1)}, u32[]{:S(2)}) copy-start(s32[3]{0:T(128)S(1)} %pad_add_fusion.place_ref) | copy-start | bytes 40
  12.4 17.1 %collective-permute-start = (bf16[192,768]{1,0:T(8,128)(2,1)S(1)}, bf16[192,768]{1,0:T(8,128)(2,1)S(1)}, u32[]{:S(2)}, u32[]{:S(2)}) collective-permute-start(bf16[192,768]{1,0:T(8,128)(2,1)S(1)} %get-tuple-element.20), channel_id=1, source_target_pairs={{0,2},{2,0},{4,6},{6,4},{8,10},{10,8},{12,14},{14,12},{16,18},{18,... | collective-permute-start | bytes 884744 | tf_op jit(solution)/shard_map/ppermute | solution.py:391
  12.9 16.6 %collective-permute-start.1 = (bf16[192,768]{1,0:T(8,128)(2,1)S(1)}, bf16[192,768]{1,0:T(8,128)(2,1)S(1)}, u32[]{:S(2)}, u32[]{:S(2)}) collective-permute-start(bf16[192,768]{1,0:T(8,128)(2,1)S(1)} %get-tuple-element.21), channel_id=1, source_target_pairs={{0,4},{2,6},{4,0},{6,2},{8,12},{10,14},{12,8},{14,10},{16,20},{18,... | collective-permute-start | bytes 884744 | tf_op jit(solution)/shard_map/ppermute | solution.py:391
  15.5 14.1 %collective-permute-start.2 = (bf16[192,768]{1,0:T(8,128)(2,1)S(1)}, bf16[192,768]{1,0:T(8,128)(2,1)S(1)}, u32[]{:S(2)}, u32[]{:S(2)}) collective-permute-start(bf16[192,768]{1,0:T(8,128)(2,1)S(1)} %get-tuple-element.22), channel_id=1, source_target_pairs={{0,6},{2,4},{4,2},{6,0},{8,14},{10,12},{12,10},{14,8},{16,22},{18,... | collective-permute-start | bytes 884744 | tf_op jit(solution)/shard_map/ppermute | solution.py:391
  15.6 2.1 collective-permute-start.3
  15.7 13.8 %collective-permute-start.4 = (f32[8,64]{1,0:T(8,128)S(1)}, f32[8,64]{1,0:T(8,128)S(1)}, u32[]{:S(2)}, u32[]{:S(2)}) collective-permute-start(f32[8,64]{1,0:T(8,128)S(1)} %get-tuple-element.25), channel_id=1, source_target_pairs={{0,4},{2,6},{4,0},{6,2},{8,12},{10,14},{12,8},{14,10},{16,20},{18,... | collective-permute-start | bytes 6152 | tf_op jit(solution)/shard_map/ppermute | solution.py:391
  17.7 11.9 %collective-permute-start.5 = (f32[8,64]{1,0:T(8,128)S(1)}, f32[8,64]{1,0:T(8,128)S(1)}, u32[]{:S(2)}, u32[]{:S(2)}) collective-permute-start(f32[8,64]{1,0:T(8,128)S(1)} %get-tuple-element.26), channel_id=1, source_target_pairs={{0,6},{2,4},{4,2},{6,0},{8,14},{10,12},{12,10},{14,8},{16,22},{18,... | collective-permute-start | bytes 6152 | tf_op jit(solution)/shard_map/ppermute | solution.py:391
  32.3 10.3 %collective-permute-start.6 = (bf16[6,144,128]{2,1,0:T(8,128)(2,1)S(1)}, bf16[6,144,128]{2,1,0:T(8,128)(2,1)S(1)}, u32[]{:S(2)}, u32[]{:S(2)}) collective-permute-start(bf16[6,144,128]{2,1,0:T(8,128)(2,1)S(1)} %get-tuple-element.27.refs_0_), channel_id=1, source_target_pairs={{0,8},{2,10},{4,12},{6,14},{8,16},{10,18},{12,20},{14,22},{16,24},... | collective-permute-start | bytes 663560 | tf_op jit(solution)/shard_map/ppermute | solution.py:395
  34.2 17.3 %collective-permute-start.7 = (bf16[6,144,128]{2,1,0:T(8,128)(2,1)S(1)}, bf16[6,144,128]{2,1,0:T(8,128)(2,1)S(1)}, u32[]{:S(2)}, u32[]{:S(2)}) collective-permute-start(bf16[6,144,128]{2,1,0:T(8,128)(2,1)S(1)} %get-tuple-element.27.refs_0_), channel_id=1, source_target_pairs={{0,16},{2,18},{4,20},{6,22},{8,24},{10,26},{12,28},{14,30},{16,0},... | collective-permute-start | bytes 663560 | tf_op jit(solution)/shard_map/ppermute | solution.py:395
  36.8 14.8 %collective-permute-start.8 = (bf16[6,144,128]{2,1,0:T(8,128)(2,1)S(1)}, bf16[6,144,128]{2,1,0:T(8,128)(2,1)S(1)}, u32[]{:S(2)}, u32[]{:S(2)}) collective-permute-start(bf16[6,144,128]{2,1,0:T(8,128)(2,1)S(1)} %get-tuple-element.27.refs_0_), channel_id=1, source_target_pairs={{0,24},{2,26},{4,28},{6,30},{8,0},{10,2},{12,4},{14,6},{16,8},{18,... | collective-permute-start | bytes 663560 | tf_op jit(solution)/shard_map/ppermute | solution.py:395
  51.6 1.4 copy-start.1
  53.0 0.7 copy-start.6
  55.2 5.6 %collective-permute-start.11 = (bf16[272,256]{1,0:T(8,128)(2,1)S(1)}, bf16[272,256]{1,0:T(8,128)(2,1)S(1)}, u32[]{:S(2)}, u32[]{:S(2)}) collective-permute-start(bf16[272,256]{1,0:T(8,128)(2,1)S(1)} %get-tuple-element.34), channel_id=1, source_target_pairs={{0,1},{1,0},{2,3},{3,2},{4,5},{5,4},{6,7},{7,6},{8,9},{9,8},{10,11... | collective-permute-start | bytes 417800 | tf_op jit(solution)/shard_map/ppermute | solution.py:508
  61.5 107.0 %all-gather.9.cloned.1.call-start = ((), (), s32[]{:S(2)}) async-start(), calls=%async_computation.1 | async-start | bytes 4456448 | tf_op jit(solution)/shard_map/all_gather | solution.py:514
  61.5 5.0 %collective-permute-start.10 = (bf16[256,256]{1,0:T(8,128)(2,1)S(1)}, bf16[256,256]{1,0:T(8,128)(2,1)S(1)}, u32[]{:S(2)}, u32[]{:S(2)}) collective-permute-start(bf16[256,256]{1,0:T(8,128)(2,1)S(1)} %get-tuple-element.33), channel_id=1, source_target_pairs={{0,1},{1,0},{2,3},{3,2},{4,5},{5,4},{6,7},{7,6},{8,9},{9,8},{10,11... | collective-permute-start | bytes 393224 | tf_op jit(solution)/shard_map/ppermute | solution.py:508
  67.3 152.5 %all-gather.7.cloned.1.call-start = ((), (), s32[]{:S(2)}) async-start(), calls=%async_computation | async-start | bytes 4456448 | tf_op jit(solution)/shard_map/all_gather | solution.py:514
  67.6 5.0 %collective-permute-start.9 = (bf16[256,256]{1,0:T(8,128)(2,1)S(1)}, bf16[256,256]{1,0:T(8,128)(2,1)S(1)}, u32[]{:S(2)}, u32[]{:S(2)}) collective-permute-start(bf16[256,256]{1,0:T(8,128)(2,1)S(1)} %get-tuple-element.32), channel_id=1, source_target_pairs={{0,1},{1,0},{2,3},{3,2},{4,5},{5,4},{6,7},{7,6},{8,9},{9,8},{10,11... | collective-permute-start | bytes 393224 | tf_op jit(solution)/shard_map/ppermute | solution.py:508
  73.4 2.8 %collective-permute-start.12 = (f32[6,8,128]{2,1,0:T(8,128)S(1)}, f32[6,8,128]{2,1,0:T(8,128)S(1)}, u32[]{:S(2)}, u32[]{:S(2)}) collective-permute-start(f32[6,8,128]{2,1,0:T(8,128)S(1)} %get-tuple-element.39), channel_id=1, source_target_pairs={{0,2},{2,0},{4,6},{6,4},{8,10},{10,8},{12,14},{14,12},{16,18},{18,... | collective-permute-start | bytes 73736 | tf_op jit(solution)/shard_map/ppermute | solution.py:391
  73.5 4.2 %collective-permute-start.13 = (f32[6,8,128]{2,1,0:T(8,128)S(1)}, f32[6,8,128]{2,1,0:T(8,128)S(1)}, u32[]{:S(2)}, u32[]{:S(2)}) collective-permute-start(f32[6,8,128]{2,1,0:T(8,128)S(1)} %get-tuple-element.38), channel_id=1, source_target_pairs={{0,4},{2,6},{4,0},{6,2},{8,12},{10,14},{12,8},{14,10},{16,20},{18,... | collective-permute-start | bytes 73736 | tf_op jit(solution)/shard_map/ppermute | solution.py:391
  75.1 3.9 %collective-permute-start.14 = (f32[6,8,128]{2,1,0:T(8,128)S(1)}, f32[6,8,128]{2,1,0:T(8,128)S(1)}, u32[]{:S(2)}, u32[]{:S(2)}) collective-permute-start(f32[6,8,128]{2,1,0:T(8,128)S(1)} %get-tuple-element.37), channel_id=1, source_target_pairs={{0,6},{2,4},{4,2},{6,0},{8,14},{10,12},{12,10},{14,8},{16,22},{18,... | collective-permute-start | bytes 73736 | tf_op jit(solution)/shard_map/ppermute | solution.py:391
  76.2 43.3 %copy-start = (bf16[4,320,256]{2,1,0:T(8,128)(2,1)}, bf16[4,320,256]{2,1,0:T(8,128)(2,1)S(1)}, u32[]{:S(2)}) copy-start(bf16[4,320,256]{2,1,0:T(8,128)(2,1)S(1)} %select_rows.1.select_ref) | copy-start | bytes 1966084
Sparse Core Ops, SparseCore 0:
  61.6 55.3 all-gather.10
  119.2 49.1 all-gather.8
  170.6 49.1 all-gather.6
